TPU v7x, 32 devices: a whole 2x2x4 slice. The times are simulated.
32 devices in a mesh: groups: 2 (over x), mx: 16 (over z, y, core).
Axes of the slice: x: 2, y: 2, z: 4, core: 2. Of those that a mesh axis runs over, the one named last changes fastest.
Arguments:
- tokens: bfloat16 [128, 18432], P('groups', 'mx'), parts along dimension 0
- norm_gain: bfloat16 [18432], P('mx'), may hold values from 0.099609375 to 1.8984375
- w_qkv: bfloat16 [18432, 8192], P(None, 'mx'), may hold values from -0.046875 to 0.046875
- key_cache: bfloat16 [128, 1024, 256], P(('groups', 'mx')), parts along dimension 0
- value_cache: bfloat16 [128, 1024, 256], P(('groups', 'mx')), parts along dimension 0, may hold values from -6 to 6
- lengths: int32 [128], P(('groups', 'mx')), parts along dimension 0, may hold values from 1 to 1024, as said below
- positions: int32 [128], P(('groups', 'mx')), parts along dimension 0, may hold values from 0 to 1023
- w_out: bfloat16 [7680, 18432], P(None, 'mx'), may hold values from -0.0625 to 0.0625
Outputs:
- mixed: bfloat16 [128, 18432], P('groups', 'mx'), parts along dimension 0
There are 2 independent parts, one for each index of `groups`. A program takes and returns all parts, laid end to end along the dimension named above; an argument that names none is the same for every part. Nothing has to cross between parts.
Inputs may be any that keep to these rules, and one draw needn't show every extreme that they name: Each row attends to its first lengths cache slots; in every draw some row has exactly 1024.
All inputs are finite; a program needn't handle non-finite values.
Results may differ from a plain program's by a relative error of at most 0.0075.
The roundings to bfloat16 on the way count: a program that leaves them out, or rounds other values in their place, can miss the bound.
Values may be sent and summed in bfloat16 or wider, within the bound.
A program may use at most 128 MiB of HBM per device.

v0:
```python
import math

import jax
import jax.numpy as jnp
from jax import lax
from jax.sharding import PartitionSpec as P

D = 18432
HQ = 30
DH = 256


epsilon = 1e-06


def rotary(vectors, position):
    half_size = vectors.shape[-1] // 2
    exponent = jnp.arange(half_size, dtype=jnp.float32) * (-2.0 / vectors.shape[-1])
    inverse_freq = jnp.power(jnp.float32(10000.0), exponent)
    angles = position.astype(jnp.float32)[:, None, None] * inverse_freq[None, None, :]
    cosine = jnp.cos(angles)
    sine_part = jnp.sin(angles)
    leading = vectors[..., :half_size]
    trailing = vectors[..., half_size:]
    return jnp.concatenate(
        [leading * cosine - trailing * sine_part, trailing * cosine + leading * sine_part], axis=-1
    )


def normalize(features, gain_part, row_mean, row_var):
    scaled = (features - row_mean[:, None]) * lax.rsqrt(row_var + epsilon)[:, None]
    return (scaled * gain_part.astype(jnp.float32)[None, :]).astype(jnp.bfloat16)


def finish_softmax(scores, own_score, highest):
    weights = jnp.exp(scores - highest[:, :, None])
    own_weight = jnp.exp(own_score - highest)
    totals = jnp.sum(weights, axis=2) + own_weight
    probs = (weights / totals[:, :, None]).astype(jnp.bfloat16)
    own_prob = (own_weight / totals).astype(jnp.bfloat16)
    return (probs, own_prob)


def shards(tokens, norm_gain, w_qkv, key_cache, value_cache, lengths, positions, w_out):
    gathered, gain_all = (
        lax.all_gather(tokens, "mx", axis=1, tiled=True),
        lax.all_gather(norm_gain, "mx", axis=0, tiled=True),
    )
    all_values = gathered.astype(jnp.float32)
    row_mean = jnp.sum(all_values, axis=1) / D
    row_var = jnp.sum(all_values * all_values, axis=1) / D - row_mean * row_mean
    normed = normalize(all_values, gain_all, row_mean, row_var)
    joined = jnp.dot(normed, w_qkv, preferred_element_type=jnp.float32)
    joined = joined.astype(jnp.bfloat16)
    own_rows = lax.all_to_all(joined, "mx", split_axis=0, concat_axis=1, tiled=True)
    local_rows = own_rows.shape[0]
    queries = rotary(
        own_rows[:, : HQ * DH].astype(jnp.float32).reshape(local_rows, HQ, DH), positions
    ).astype(jnp.bfloat16)
    new_key = (
        rotary(
            own_rows[:, HQ * DH : HQ * DH + DH].astype(jnp.float32).reshape(local_rows, 1, DH),
            positions,
        )
        .astype(jnp.bfloat16)
        .reshape(local_rows, DH)
    )
    new_value = own_rows[:, HQ * DH + DH :]
    scaling = 1.0 / math.sqrt(DH)
    own_score = (
        jnp.einsum("rhd,rd->rh", queries, new_key, preferred_element_type=jnp.float32) * scaling
    )
    cache_span = key_cache.shape[1]
    scores = (
        jnp.einsum("rhd,rtd->rht", queries, key_cache, preferred_element_type=jnp.float32) * scaling
    )
    slot_ids = jnp.arange(cache_span, dtype=jnp.int32)
    live_mask = slot_ids[None, None, :] < lengths[:, None, None]
    scores = jnp.where(live_mask, scores, -jnp.inf)
    highest = jnp.maximum(jnp.max(scores, axis=2), own_score)
    probs, own_prob = finish_softmax(scores, own_score, highest)
    attended = jnp.einsum("rht,rtd->rhd", probs, value_cache, preferred_element_type=jnp.float32)
    attended = (
        attended
        + own_prob.astype(jnp.float32)[:, :, None] * new_value.astype(jnp.float32)[:, None, :]
    )
    attended = attended.astype(jnp.bfloat16).reshape(local_rows, HQ * DH)
    return jnp.dot(
        lax.all_gather(attended, "mx", axis=0, tiled=True),
        w_out,
        preferred_element_type=jnp.float32,
    ).astype(jnp.bfloat16)


def solution(mesh):
    placed = (
        P("groups", "mx"),
        P("mx"),
        P(None, "mx"),
        P(("groups", "mx"), None, None),
        P(("groups", "mx"), None, None),
        P(("groups", "mx")),
        P(("groups", "mx")),
        P(None, "mx"),
    )
    return jax.shard_map(
        shards, mesh=mesh, in_specs=placed, out_specs=P("groups", "mx"), check_vma=False
    )
```

profile of v0, /device:TPU:1, one launch (start us, length us, event | category | flops | bytes accessed | tf_op | source)
XLA Modules:
  0.0 121.2 jit_solution(16606096777755045079)
XLA Ops:
  6.5 0.0 copy-start
  6.5 0.0 all-gather.4.cloned.1.call-start
  6.5 0.7 all-gather.4.cloned.1.call-update
  7.3 0.7 reshape.184
  8.0 23.2 %all-gather = bf16[16,1,1152]{2,1,0:T(2,128)(2,1)S(1)} all-gather(bf16[1,1,1152]{2,1,0:T(2,128)(2,1)S(1)} %reshape.184), channel_id=1, replica_groups=mesh['groups'=2,'mx'=16] {'mx'}, dimensions={0}, use_global_device_ids=true | all-gather | bytes 39168 | tf_op jit(solution)/shard_map/all_gather | solution.py:47
  31.1 0.1 convert_element_type.52
  31.2 0.7 convert_element_type.45
  31.9 0.1 multiply_cosine_fusion.1
  32.0 22.6 %all-gather.4.cloned.1.call-done = bf16[64,18432]{1,0:T(8,128)(2,1)} async-done(((bf16[64,1152]{1,0:T(8,128)(2,1)}), bf16[64,18432]{1,0:T(8,128)(2,1)}) %all-gather.4.cloned.1.call-update) | async-done | bytes 2359312 | tf_op jit(solution)/shard_map/all_gather | solution.py:46
  54.6 2.4 %convert_reduce_fusion = (f32[64]{0:T(128)S(1)}, f32[64]{0:T(128)S(1)}) fusion(bf16[64,18432]{1,0:T(8,128)(2,1)} %all-gather.4.cloned.1.call-done), kind=kLoop, calls=%fused_computation.2 | loop fusion | flops 4718464 | bytes 2359808 | tf_op jit(solution)/shard_map/reduce_sum | solution.py:50
  57.0 0.0 copy-start.1
  57.0 10.5 %fusion.11 = bf16[64,512]{1,0:T(8,128)(2,1)S(1)} fusion(bf16[18432,512]{1,0:T(8,128)(2,1)} %param.10, bf16[64,18432]{1,0:T(8,128)(2,1)} %all-gather.4.cloned.1.call-done, f32[18432]{0:T(1024)S(1)} %bitcast.22, f32[64]{0:T(128)S(1)} %get-tuple-element.18, f32[64]{0:T(128)S(1)} %get-tuple-element.17), kind=kOutput, calls=%fused_computation.16 | convolution fusion | flops 1213890560 | bytes 21373440 | tf_op jit(solution)/shard_map/dot_general | solution.py:53
  67.5 0.7 all_to_all.14
  68.2 3.7 %all-to-all-start = ((bf16[16,4,512]{2,1,0:T(4,128)(2,1)}), bf16[16,4,512]{2,1,0:T(4,128)(2,1)S(1)}, u32[]{:S(2)}, u32[]{:S(2)}) async-start(bf16[16,4,512]{2,1,0:T(4,128)(2,1)} %all_to_all.14), calls=%async_computation | async-start | bytes 131072 | tf_op jit(solution)/shard_map/all_to_all | solution.py:55
  71.8 0.0 copy-done.1
  71.8 0.1 iota_compare_fusion
  71.9 6.0 %all-to-all-done = bf16[16,4,512]{2,1,0:T(4,128)(2,1)S(1)} async-done(((bf16[16,4,512]{2,1,0:T(4,128)(2,1)}), bf16[16,4,512]{2,1,0:T(4,128)(2,1)S(1)}, u32[]{:S(2)}, u32[]{:S(2)}) %all-to-all-start) | async-done | bytes 65568 | tf_op jit(solution)/shard_map/all_to_all | solution.py:55
  77.9 0.1 reshape.181
  78.0 0.1 fusion.30
  78.2 0.1 fusion.17
  78.3 0.0 copy-done
  78.3 0.8 fusion.34
  79.1 0.2 fusion.14
  79.4 2.1 %fusion.10 = bf16[4,30,256]{2,1,0:T(8,128)(2,1)S(1)} fusion(bf16[4,1024,256]{2,1,0:T(8,128)(2,1)} %param.12, f32[4,30,1024]{2,1,0:T(8,128)S(1)} %get-tuple-element.20, f32[4,30]{1,0:T(4,128)S(1)} %get-tuple-element.12, f32[4,30]{1,0:T(4,128)S(1)} %multiply_maximum_fusion, f32[4,256]{1,0:T(4,128)S(1)} %get-tuple-element.9, f32[4,30]{1,0:T(4,128)S(1)} %get-tuple-element.11), kind=kOutput, calls=%fused_computation.15 | convolution fusion | flops 63375360 | bytes 2655648 | tf_op jit(solution)/shard_map/rht,rtd->rhd/dot_general | solution.py:82
  81.5 22.7 %all-gather.1 = bf16[16,4,7680]{2,1,0:T(4,128)(2,1)} all-gather(bf16[1,4,7680]{2,1,0:T(4,128)(2,1)S(1)} %reshape.186), channel_id=1, replica_groups=mesh['groups'=2,'mx'=16] {'mx'}, dimensions={0}, use_global_device_ids=true | all-gather | bytes 1044480 | tf_op jit(solution)/shard_map/all_gather | solution.py:89
  104.3 1.7 %reshape.187 = bf16[64,7680]{1,0:T(8,128)(2,1)S(1)} reshape(bf16[16,4,7680]{2,1,0:T(4,128)(2,1)} %all-gather.1) | data formatting | bytes 1966080
  106.0 8.4 %convolution_convert_fusion = bf16[64,1152]{1,0:T(8,128)(2,1)} fusion(bf16[64,7680]{1,0:T(8,128)(2,1)S(1)} %reshape.187, bf16[7680,1152]{1,0:T(8,128)(2,1)} %param.15), kind=kOutput, calls=%fused_computation.11 | convolution fusion | flops 1132535808 | bytes 18825216 | tf_op jit(solution)/shard_map/dot_general | solution.py:88
  (9 shorter events, 0.1 us)
Async XLA Ops:
  6.5 71.8 %copy-start = (bf16[4,1024,256]{2,1,0:T(8,128)(2,1)S(1)}, bf16[4,1024,256]{2,1,0:T(8,128)(2,1)}, u32[]{:S(2)}) copy-start(bf16[4,1024,256]{2,1,0:T(8,128)(2,1)} %param.11) | copy-start | bytes 6291460
  6.5 48.0 %all-gather.4.cloned.1.call-start = ((), (), s32[]{:S(2)}) async-start(), calls=%async_computation.1 | async-start | bytes 2506752 | tf_op jit(solution)/shard_map/all_gather | solution.py:46
  57.0 14.9 %copy-start.1 = (s32[4]{0:T(128)S(1)}, s32[4]{0:T(128)}, u32[]{:S(2)}) copy-start(s32[4]{0:T(128)} %param.13) | copy-start | bytes 52
  68.2 9.7 %all-to-all-start = ((bf16[16,4,512]{2,1,0:T(4,128)(2,1)}), bf16[16,4,512]{2,1,0:T(4,128)(2,1)S(1)}, u32[]{:S(2)}, u32[]{:S(2)}) async-start(bf16[16,4,512]{2,1,0:T(4,128)(2,1)} %all_to_all.14), calls=%async_computation | async-start | bytes 131072 | tf_op jit(solution)/shard_map/all_to_all | solution.py:55
Sparse Core Ops, SparseCore 0:
  9.7 44.8 all-gather.3
where the time goes:
time: 122 us; the launch traced here: 121 us
  blocking collectives  45.9 us (38%)
  waiting for transfers between devices  29.3 us (24%)
  matrix products  22 us (18%)
  between operations  13.5 us (11%)
  other arithmetic  3.73 us (3%)
  starting transfers between devices  3.69 us (3%)
  local copies, waits for them, and re-layouts  3.18 us (3%)
    all_gather x1, blocking collectives, shards(): lax.all_gather(norm_gain, 'mx', axis=0, tiled=True)  23.2 us
    all_gather x1, blocking collectives, shards(): lax.all_gather(attended, 'mx', axis=0, tiled=True)  22.7 us
    all_gather x1, waiting for transfers between devices, shards(): lax.all_gather(tokens, 'mx', axis=1, tiled=True)  22.6 us
    dot_general x1, matrix products, shards(): joined = jnp.dot(normed, w_qkv, preferred_element_type=jnp.float32)  10.5 us
    dot_general x1, matrix products, shards(): jnp.dot(lax.all_gather(attended, 'mx', axis=0, tiled=True), w_out, prefer...  8.39 us
    all_to_all x1, waiting for transfers between devices, shards(): lax.all_to_all(joined, 'mx', split_axis=0, concat_axis=1, tiled=True)  5.96 us
    all_to_all x1, starting transfers between devices, shards(): lax.all_to_all(joined, 'mx', split_axis=0, concat_axis=1, tiled=True)  3.69 us
    unnamed x7, local copies, waits for them, and re-layouts  2.44 us
  transfers between devices with their start and end apart: 2, of which 2 were waited for; matrix products, arithmetic and copies ran while one was open for 1% of the time, Pallas kernels for 0%

commit v1 on v0

v1 whole, which is shorter than its diff:
```python
import functools
import math

import jax
import jax.numpy as jnp
from jax import lax
from jax.experimental import pallas as pl
from jax.experimental.pallas import tpu as pltpu
from jax.sharding import PartitionSpec as P

D = 18432
HQ = 30
DH = 256
HALF = DH // 2
SLOTS = HQ + 2
OUT_CHUNKS = 6

epsilon = 1e-06

MESH = pl.DeviceIdType.MESH


def remote(src, dst, send_sem, recv_sem, peer):
    return pltpu.make_async_remote_copy(
        src_ref=src,
        dst_ref=dst,
        send_sem=send_sem,
        recv_sem=recv_sem,
        device_id={"mx": peer},
        device_id_type=MESH,
    )


class Gather:
    def __init__(self, n, me, buf, send_sems, recv_sems):
        self.n, self.me, self.buf = n, me, buf
        self.send_sems, self.recv_sems = send_sems, recv_sems
        self.outer = n // 4
        self.core = lax.rem(me, 2)
        self.b = lax.rem(me // 2, 2)
        self.a = me // 4
        self.used = 0
        self.sent = []

    def slab(self, k, other_b, other_core):
        a = lax.rem(self.a + self.outer - k, self.outer)
        b = 1 - self.b if other_b else self.b
        core = 1 - self.core if other_core else self.core
        return a * 4 + b * 2 + core

    def send(self, slab, peer):
        copy = remote(
            self.buf.at[slab],
            self.buf.at[slab],
            self.send_sems.at[self.used],
            self.recv_sems.at[slab],
            peer,
        )
        self.used += 1
        copy.start()
        self.sent.append(copy)

    def arrive(self, slab):
        remote(
            self.buf.at[slab],
            self.buf.at[slab],
            self.send_sems.at[0],
            self.recv_sems.at[slab],
            self.me,
        ).wait_recv()

    def to_a(self):
        for k in range(1, self.outer):
            a = lax.rem(self.a + k, self.outer)
            self.send(self.me, a * 4 + self.b * 2 + self.core)

    def to_b(self, slab):
        self.send(slab, self.a * 4 + (1 - self.b) * 2 + self.core)

    def to_core(self, slab):
        self.send(slab, self.a * 4 + self.b * 2 + 1 - self.core)

    def run(self, use):
        self.to_b(self.me)
        self.to_core(self.me)
        self.to_a()
        for k in range(self.outer):
            mine = self.slab(k, False, False)
            if k:
                self.arrive(mine)
                self.to_b(mine)
                self.to_core(mine)
            use(mine)
            across = self.slab(k, True, False)
            self.arrive(across)
            self.to_core(across)
            use(across)
            for other_b in (False, True):
                slab = self.slab(k, other_b, True)
                self.arrive(slab)
                use(slab)

    def finish(self):
        for copy in self.sent:
            copy.wait_send()


def n_gather_sends(n):
    return (n // 4 - 1) + n // 4 + n // 2


def kernel(
    n, x_ref, gain_ref, w_hbm, k_hbm, v_hbm, len_ref, cos_ref, sin_ref, wo_hbm, out_ref,
    stats, xg, w_v, acc, joined_out, joined_in, joined_2d, k_v, v_v, heads_first, att,
    att_2d, wo_v, total,
    w_sems, kv_sems, wo_sems, st_send, st_recv, x_send, x_recv, j_send, j_recv, a_send, a_recv,
):
    me = lax.axis_index("mx")
    rows, features = x_ref.shape
    columns = w_hbm.shape[1]
    local = k_hbm.shape[0]
    context = k_hbm.shape[1]

    barrier = pltpu.get_barrier_semaphore()

    def greet(k, carry):
        pl.semaphore_signal(
            barrier, inc=1, device_id={"mx": lax.rem(me + k, n)}, device_id_type=MESH
        )
        return carry

    lax.fori_loop(1, n, greet, 0)

    gather = Gather(n, me, xg, x_send, x_recv)

    def w_copy(slab):
        start = pl.multiple_of(slab * features, features)
        return pltpu.make_async_copy(
            w_hbm.at[pl.ds(start, features), :], w_v.at[slab], w_sems.at[slab]
        )

    for k in range(gather.outer):
        for other_core in (False, True):
            for other_b in (False, True):
                w_copy(gather.slab(k, other_b, other_core)).start()
    k_copy = pltpu.make_async_copy(k_hbm, k_v, kv_sems.at[0])
    v_copy = pltpu.make_async_copy(v_hbm, v_v, kv_sems.at[1])
    k_copy.start()
    v_copy.start()
    depth = wo_hbm.shape[0] // OUT_CHUNKS
    wo_copies = [
        pltpu.make_async_copy(
            wo_hbm.at[pl.ds(i * depth, depth), :], wo_v.at[i], wo_sems.at[i]
        )
        for i in range(OUT_CHUNKS)
    ]
    for copy in wo_copies:
        copy.start()

    x = x_ref[...].astype(jnp.float32)
    eye = lax.broadcasted_iota(jnp.int32, (rows, rows), 0) == lax.broadcasted_iota(
        jnp.int32, (rows, rows), 1
    )

    def as_row(column):
        return jnp.sum(jnp.where(eye, column, 0.0), axis=0, keepdims=True)

    def as_column(row):
        return jnp.sum(jnp.where(eye, row, 0.0), axis=1, keepdims=True)

    stats[me, 0:1, :] = as_row(jnp.sum(x, axis=1, keepdims=True))
    stats[me, 1:2, :] = as_row(jnp.sum(x * x, axis=1, keepdims=True))

    pl.semaphore_wait(barrier, n - 1)

    def st_copy(k):
        return remote(
            stats.at[me], stats.at[me], st_send.at[k], st_recv.at[me], lax.rem(me + k, n)
        )

    def start_stats(k, carry):
        st_copy(k).start()
        return carry

    def wait_stats(k, carry):
        source = lax.rem(me + k, n)
        remote(
            stats.at[source], stats.at[source], st_send.at[k], st_recv.at[source], me
        ).wait_recv()
        return carry

    lax.fori_loop(1, n, start_stats, 0)
    acc[...] = jnp.zeros_like(acc)
    lax.fori_loop(1, n, wait_stats, 0)
    sums = jnp.sum(stats[...], axis=0)
    row_mean = sums[0:1, :] / D
    row_var = sums[1:2, :] / D - row_mean * row_mean
    scale = as_column(lax.rsqrt(row_var + epsilon))
    shift = as_column(row_mean)
    xg[me] = ((x - shift) * scale * gain_ref[...].astype(jnp.float32)).astype(jnp.bfloat16)

    def project(slab):
        w_copy(slab).wait()
        acc[...] += jnp.dot(xg[slab], w_v[slab], preferred_element_type=jnp.float32)

    gather.run(project)

    for j in range(n):
        joined_out[j] = acc[j * local : (j + 1) * local, :].astype(jnp.bfloat16)
    joined_in[me] = joined_out[me]

    def j_copy(k):
        peer = lax.rem(me + k, n)
        return remote(
            joined_out.at[peer], joined_in.at[me], j_send.at[k], j_recv.at[me], peer
        )

    def start_joined(k, carry):
        j_copy(k).start()
        return carry

    def wait_joined(k, carry):
        source = lax.rem(me + k, n)
        remote(
            joined_out.at[source], joined_in.at[source], j_send.at[k], j_recv.at[source], me
        ).wait_recv()
        return carry

    lax.fori_loop(1, n, start_joined, 0)
    lax.fori_loop(1, n, wait_joined, 0)
    for j in range(n):
        joined_2d[j * local : (j + 1) * local, :] = joined_in[j].astype(jnp.float32)

    pieces = columns // HALF
    shape = (local * SLOTS, n * local)
    to_row = lax.broadcasted_iota(jnp.int32, shape, 0)
    from_row = lax.broadcasted_iota(jnp.int32, shape, 1)
    same_row = to_row // SLOTS == from_row % local
    to_piece = 2 * (to_row % SLOTS)
    from_piece = pieces * (from_row // local)
    halves = []
    for part in range(2):
        half = jnp.zeros((local * SLOTS, HALF), jnp.float32)
        for piece in range(pieces):
            if pieces % 2 == 0 and piece % 2 != part:
                continue
            chosen = same_row & (from_piece + piece == to_piece + part)
            half += jnp.dot(
                jnp.where(chosen, 1.0, 0.0).astype(jnp.bfloat16),
                joined_2d[:, piece * HALF : (piece + 1) * HALF].astype(jnp.bfloat16),
                preferred_element_type=jnp.float32,
            )
        halves.append(half)

    k_copy.wait()
    v_copy.wait()
    scaling = 1.0 / math.sqrt(DH)
    slot_ids = lax.broadcasted_iota(jnp.int32, (SLOTS, context), 1)
    results = []
    for r in range(local):
        leading = halves[0][r * SLOTS : (r + 1) * SLOTS]
        trailing = halves[1][r * SLOTS : (r + 1) * SLOTS]
        cosine = cos_ref[r : r + 1, :]
        sine = sin_ref[r : r + 1, :]
        rotated = jnp.concatenate(
            [leading * cosine - trailing * sine, trailing * cosine + leading * sine], axis=1
        ).astype(jnp.bfloat16)
        new_value = jnp.concatenate(
            [leading[SLOTS - 1 : SLOTS], trailing[SLOTS - 1 : SLOTS]], axis=1
        )
        wide = rotated.astype(jnp.float32)
        own = jnp.sum(wide * wide[HQ : HQ + 1], axis=1, keepdims=True) * scaling
        scores = (
            lax.dot_general(
                rotated, k_v[r], (((1,), (1,)), ((), ())), preferred_element_type=jnp.float32
            )
            * scaling
        )
        scores = jnp.where(slot_ids < len_ref[r], scores, -jnp.inf)
        highest = jnp.maximum(jnp.max(scores, axis=1, keepdims=True), own)
        weights = jnp.exp(scores - highest)
        own_weight = jnp.exp(own - highest)
        totals = jnp.sum(weights, axis=1, keepdims=True) + own_weight
        inverse = 1.0 / totals
        probs = (weights * inverse).astype(jnp.bfloat16)
        own_prob = (own_weight * inverse).astype(jnp.bfloat16).astype(jnp.float32)
        attended = jnp.dot(probs, v_v[r], preferred_element_type=jnp.float32)
        results.append((attended + own_prob * new_value).astype(jnp.bfloat16))
    stacked = jnp.concatenate(results, axis=0)

    square = (local * SLOTS, local * SLOTS)
    to_row = lax.broadcasted_iota(jnp.int32, square, 0)
    from_row = lax.broadcasted_iota(jnp.int32, square, 1)
    swap = (to_row // local == from_row % SLOTS) & (to_row % local == from_row // SLOTS)
    heads_first[...] = jnp.dot(
        jnp.where(swap, 1.0, 0.0).astype(jnp.bfloat16),
        stacked,
        preferred_element_type=jnp.float32,
    )
    for h in range(HQ):
        att[me, :, h * DH : (h + 1) * DH] = heads_first[
            h * local : (h + 1) * local, :
        ].astype(jnp.bfloat16)

    spread = Gather(n, me, att, a_send, a_recv)
    spread.run(lambda slab: None)

    for j in range(n):
        att_2d[j * local : (j + 1) * local, :] = att[j].astype(jnp.float32)
    for i, copy in enumerate(wo_copies):
        copy.wait()
        product = jnp.dot(
            att_2d[:, i * depth : (i + 1) * depth].astype(jnp.bfloat16),
            wo_v[i],
            preferred_element_type=jnp.float32,
        )
        if i == 0:
            total[...] = product
        elif i < OUT_CHUNKS - 1:
            total[...] += product
        else:
            out_ref[...] = (total[...] + product).astype(jnp.bfloat16)

    def finish(k, carry):
        st_copy(k).wait_send()
        j_copy(k).wait_send()
        return carry

    lax.fori_loop(1, n, finish, 0)
    gather.finish()
    spread.finish()


def shards(n, tokens, norm_gain, w_qkv, key_cache, value_cache, lengths, positions, w_out):
    rows, features = tokens.shape
    columns = w_qkv.shape[1]
    local, context, _ = key_cache.shape
    inner, width = w_out.shape
    exponent = jnp.arange(HALF, dtype=jnp.float32) * (-2.0 / DH)
    inverse_freq = jnp.power(jnp.float32(10000.0), exponent)
    angles = positions.astype(jnp.float32)[:, None] * inverse_freq[None, :]
    bf16, f32 = jnp.bfloat16, jnp.float32
    vmem = pl.BlockSpec(memory_space=pltpu.VMEM)
    smem = pl.BlockSpec(memory_space=pltpu.SMEM)
    hbm = pl.BlockSpec(memory_space=pl.ANY)
    dma = pltpu.SemaphoreType.DMA
    sends = n_gather_sends(n)
    return pl.pallas_call(
        functools.partial(kernel, n),
        out_shape=jax.ShapeDtypeStruct((rows, width), bf16),
        in_specs=[vmem, vmem, hbm, hbm, hbm, smem, vmem, vmem, hbm],
        out_specs=vmem,
        scratch_shapes=[
            pltpu.VMEM((n, 2, rows), f32),
            pltpu.VMEM((n, rows, features), bf16),
            pltpu.VMEM((n, features, columns), bf16),
            pltpu.VMEM((rows, columns), f32),
            pltpu.VMEM((n, local, columns), bf16),
            pltpu.VMEM((n, local, columns), bf16),
            pltpu.VMEM((rows, columns), f32),
            pltpu.VMEM((local, context, DH), bf16),
            pltpu.VMEM((local, context, DH), bf16),
            pltpu.VMEM((local * SLOTS, DH), f32),
            pltpu.VMEM((n, local, inner), bf16),
            pltpu.VMEM((rows, inner), f32),
            pltpu.VMEM((OUT_CHUNKS, inner // OUT_CHUNKS, width), bf16),
            pltpu.VMEM((rows, width), f32),
            dma((n,)),
            dma((2,)),
            dma((OUT_CHUNKS,)),
            dma((n,)),
            dma((n,)),
            dma((sends,)),
            dma((n,)),
            dma((n,)),
            dma((n,)),
            dma((sends,)),
            dma((n,)),
        ],
        compiler_params=pltpu.CompilerParams(
            collective_id=0, has_side_effects=True, vmem_limit_bytes=60 * 1024 * 1024
        ),
    )(
        tokens, norm_gain.reshape(1, features), w_qkv, key_cache, value_cache, lengths,
        jnp.cos(angles), jnp.sin(angles), w_out,
    )


def solution(mesh):
    placed = (
        P("groups", "mx"),
        P("mx"),
        P(None, "mx"),
        P(("groups", "mx"), None, None),
        P(("groups", "mx"), None, None),
        P(("groups", "mx")),
        P(("groups", "mx")),
        P(None, "mx"),
    )
    return jax.shard_map(
        functools.partial(shards, mesh.shape["mx"]),
        mesh=mesh,
        in_specs=placed,
        out_specs=P("groups", "mx"),
        check_vma=False,
    )
```

time: 122 us -> 73.1 us (0.60)
  Pallas kernels: 0 us -> 68.7 us
  blocking collectives: 45.9 us -> 0 us
  waiting for transfers between devices: 29.3 us -> 0 us
  matrix products: 22 us -> 0 us
  between operations: 13.5 us -> 0.01 us
  starting transfers between devices: 3.69 us -> 0 us
  other arithmetic: 3.73 us -> 1.36 us
    pallas_call x0 -> x1, Pallas kernels: none -> 68.7 us  [shards(): pl.pallas_call(functools.partial(kernel, n), out_shape=jax.ShapeDtypeStru...]
    all_gather x2 -> x0, blocking collectives: 45.9 us -> none  [the longest x1 23.2 us: shards(): lax.all_gather(norm_gain, 'mx', axis=0, tiled=True)]
    all_gather x1 -> x0, waiting for transfers between devices: 22.6 us -> none  [shards(): lax.all_gather(tokens, 'mx', axis=1, tiled=True)]
    dot_general x5 -> x0, matrix products: 22 us -> none  [the longest x1 10.5 us: shards(): joined = jnp.dot(normed, w_qkv, preferred_element_type=jnp.float32)]
    all_to_all x1 -> x0, waiting for transfers between devices: 5.96 us -> none  [shards(): lax.all_to_all(joined, 'mx', split_axis=0, concat_axis=1, tiled=True)]
    all_to_all x1 -> x0, starting transfers between devices: 3.69 us -> none  [shards(): lax.all_to_all(joined, 'mx', split_axis=0, concat_axis=1, tiled=True)]
    reduce_sum x2 -> x0, other arithmetic: 2.6 us -> none  [the longest x1 2.37 us: shards(): row_mean = jnp.sum(all_values, axis=1) / D]
    unnamed x7 -> x1, local copies, waits for them, and re-layouts: 2.44 us -> 1.58 us
  transfers between devices with their start and end apart: 2 -> 0, of which waited for: 2 -> 0; matrix products, arithmetic and copies ran while one was open for 1% -> 0% of each run, Pallas kernels for 0% -> 0%
where the time goes in v1:
time: 73.1 us; the launch traced here: 72.9 us
  Pallas kernels  68.7 us (94%)
  local copies, waits for them, and re-layouts  2.87 us (4%)
  other arithmetic  1.36 us (2%)
    pallas_call x1, Pallas kernels, shards(): pl.pallas_call(functools.partial(kernel, n), out_shape=jax.ShapeDtypeStru...  68.7 us
    unnamed x1, local copies, waits for them, and re-layouts  1.58 us

profile of v1, /device:TPU:1, one launch (start us, length us, event | category | flops | bytes accessed | tf_op | source)
XLA Modules:
  0.0 72.9 jit_solution(17518554865115669459)
XLA Ops:
  0.0 0.7 convert_element_type.3
  0.7 0.7 multiply_sine_fusion
  1.4 1.3 %reshape.9.gain_ref = bf16[1,1152]{1,0:T(2,128)(2,1)} reshape(bf16[1152]{0:T(1024)(128)(2,1)} %param.9) | data formatting | bytes 4608 | tf_op jit(solution)/shard_map/reshape | solution.py:384
  2.6 68.7 %shard_map.82 = bf16[64,1152]{1,0:T(8,128)(2,1)} custom-call(bf16[64,1152]{1,0:T(8,128)(2,1)} %x_ref.1, bf16[1,1152]{1,0:T(2,128)(2,1)} %reshape.9.gain_ref, bf16[18432,512]{1,0:T(8,128)(2,1)} %w_hbm.1, bf16[4,1024,256]{2,1,0:T(8,128)(2,1)} %k_hbm.1, bf16[4,1024,256]{2,1,0:T(8,128)(2,1)} %v_hbm.1, s32[4]{0:T(128)} %len_ref.1, ...), custom_call_target="tpu_custom_call" | custom-call | tf_op jit(solution)/shard_map/pallas_call | solution.py:348
  71.3 1.6 %copy.10 = bf16[64,1152]{1,0:T(8,128)(2,1)} copy(bf16[64,1152]{1,0:T(8,128)(2,1)} %shard_map.82) | data formatting | bytes 294912
  (1 shorter events, 0.0 us)

commit v2 on v1

--- a/solution.py
+++ b/solution.py
@@ -13,7 +13,8 @@
 DH = 256
 HALF = DH // 2
 SLOTS = HQ + 2
-OUT_CHUNKS = 6
+OUT_CHUNKS = 4
+X_CHUNKS = 2
 
 epsilon = 1e-06
 
@@ -32,87 +33,113 @@
 
 
 class Gather:
-    def __init__(self, n, me, buf, send_sems, recv_sems):
+    def __init__(self, n, me, buf, chunks, send_sems, recv_sems):
         self.n, self.me, self.buf = n, me, buf
         self.send_sems, self.recv_sems = send_sems, recv_sems
         self.outer = n // 4
         self.core = lax.rem(me, 2)
         self.b = lax.rem(me // 2, 2)
         self.a = me // 4
-        self.used = 0
-        self.sent = []
-
-    def slab(self, k, other_b, other_core):
-        a = lax.rem(self.a + self.outer - k, self.outer)
+        self.chunks = chunks
+        self.depth = buf.shape[1] // chunks
+
+    def index(self, a, other_b, other_core):
         b = 1 - self.b if other_b else self.b
         core = 1 - self.core if other_core else self.core
         return a * 4 + b * 2 + core
 
-    def send(self, slab, peer):
-        copy = remote(
-            self.buf.at[slab],
-            self.buf.at[slab],
-            self.send_sems.at[self.used],
-            self.recv_sems.at[slab],
-            peer,
-        )
-        self.used += 1
-        copy.start()
-        self.sent.append(copy)
-
-    def arrive(self, slab):
-        remote(
-            self.buf.at[slab],
-            self.buf.at[slab],
-            self.send_sems.at[0],
-            self.recv_sems.at[slab],
-            self.me,
-        ).wait_recv()
-
-    def to_a(self):
-        for k in range(1, self.outer):
-            a = lax.rem(self.a + k, self.outer)
-            self.send(self.me, a * 4 + self.b * 2 + self.core)
-
-    def to_b(self, slab):
-        self.send(slab, self.a * 4 + (1 - self.b) * 2 + self.core)
-
-    def to_core(self, slab):
-        self.send(slab, self.a * 4 + self.b * 2 + 1 - self.core)
+    def copy(self, slab, chunk, kind, peer):
+        part = self.buf.at[slab, pl.ds(chunk * self.depth, self.depth), :]
+        return remote(
+            part, part, self.send_sems.at[kind, slab, chunk], self.recv_sems.at[slab, chunk], peer
+        )
+
+    def out(self, a, chunk, kind, other_b=False, wait=False):
+        slab = self.index(a, other_b, False)
+        ahead = {0: self.a - 1, 1: self.a + 1}.get(kind, self.a)
+        peer = self.index(ahead, kind == 2, kind == 3)
+
+        def go():
+            copy = self.copy(slab, chunk, kind, peer)
+            if wait:
+                copy.wait_send()
+            else:
+                copy.start()
+
+        if kind == 0:
+            pl.when((self.a > 0) & (a >= self.a))(go)
+        elif kind == 1:
+            pl.when((self.a < self.outer - 1) & (a <= self.a))(go)
+        else:
+            go()
+
+    def arrive(self, slab, chunk):
+        self.copy(slab, chunk, 0, self.me).wait_recv()
+
+    def order(self):
+        for step in range(1, self.outer):
+            yield self.a - step, self.a - step >= 0
+            yield self.a + step, self.a + step < self.outer
+
+    def each(self, act):
+        act(self.a)
+        for a, there in self.order():
+            pl.when(there)(functools.partial(act, a))
 
     def run(self, use):
-        self.to_b(self.me)
-        self.to_core(self.me)
-        self.to_a()
-        for k in range(self.outer):
-            mine = self.slab(k, False, False)
-            if k:
-                self.arrive(mine)
-                self.to_b(mine)
-                self.to_core(mine)
-            use(mine)
-            across = self.slab(k, True, False)
-            self.arrive(across)
-            self.to_core(across)
-            use(across)
+        def forward(a, chunk):
+            for kind in (0, 1, 2, 3):
+                self.out(a, chunk, kind)
+
+        for chunk in range(self.chunks):
+            forward(self.a, chunk)
+
+        def mine(a):
+            for chunk in range(self.chunks):
+                self.arrive(self.index(a, False, False), chunk)
+                forward(a, chunk)
+
+        def across(a):
+            for chunk in range(self.chunks):
+                self.arrive(self.index(a, True, False), chunk)
+                self.out(a, chunk, 3, other_b=True)
+
+        def beside(a):
             for other_b in (False, True):
-                slab = self.slab(k, other_b, True)
-                self.arrive(slab)
+                slab = self.index(a, other_b, True)
+                for chunk in range(self.chunks):
+                    self.arrive(slab, chunk)
                 use(slab)
 
+        def settle(a):
+            across(a)
+            use(self.index(a, False, False))
+            use(self.index(a, True, False))
+            beside(a)
+
+        places = list(self.order())
+        for step in range(self.outer):
+            for a, there in places[2 * step : 2 * step + 2]:
+                pl.when(there)(functools.partial(mine, a))
+            if step == 0:
+                settle(self.a)
+            for a, there in places[2 * step - 2 : 2 * step] if step else []:
+                pl.when(there)(functools.partial(settle, a))
+
     def finish(self):
-        for copy in self.sent:
-            copy.wait_send()
-
-
-def n_gather_sends(n):
-    return (n // 4 - 1) + n // 4 + n // 2
+        def act(a):
+            for chunk in range(self.chunks):
+                for kind in (0, 1, 2, 3):
+                    self.out(a, chunk, kind, wait=True)
+                self.out(a, chunk, 3, other_b=True, wait=True)
+
+        self.each(act)
 
 
 def kernel(
     n, x_ref, gain_ref, w_hbm, k_hbm, v_hbm, len_ref, cos_ref, sin_ref, wo_hbm, out_ref,
-    stats, xg, w_v, acc, joined_out, joined_in, joined_2d, k_v, v_v, heads_first, att,
-    att_2d, wo_v, total,
+    stats, xg, w_v, acc, joined_f32, joined_out, joined_in, joined_2d, k_v, v_v, heads_first,
+    att_f32, att, wo_v, total,
     w_sems, kv_sems, wo_sems, st_send, st_recv, x_send, x_recv, j_send, j_recv, a_send, a_recv,
 ):
     me = lax.axis_index("mx")
@@ -131,7 +158,7 @@
 
     lax.fori_loop(1, n, greet, 0)
 
-    gather = Gather(n, me, xg, x_send, x_recv)
+    gather = Gather(n, me, xg, X_CHUNKS, x_send, x_recv)
 
     def w_copy(slab):
         start = pl.multiple_of(slab * features, features)
@@ -139,10 +166,12 @@
             w_hbm.at[pl.ds(start, features), :], w_v.at[slab], w_sems.at[slab]
         )
 
-    for k in range(gather.outer):
+    def fetch(a):
         for other_core in (False, True):
             for other_b in (False, True):
-                w_copy(gather.slab(k, other_b, other_core)).start()
+                w_copy(gather.index(a, other_b, other_core)).start()
+
+    gather.each(fetch)
     k_copy = pltpu.make_async_copy(k_hbm, k_v, kv_sems.at[0])
     v_copy = pltpu.make_async_copy(v_hbm, v_v, kv_sems.at[1])
     k_copy.start()
@@ -205,8 +234,13 @@
 
     gather.run(project)
 
+    pieces = columns // HALF
     for j in range(n):
-        joined_out[j] = acc[j * local : (j + 1) * local, :].astype(jnp.bfloat16)
+        for piece in range(pieces):
+            joined_f32[j, piece * local : (piece + 1) * local, :] = acc[
+                j * local : (j + 1) * local, piece * HALF : (piece + 1) * HALF
+            ]
+    joined_out[...] = joined_f32[...].astype(jnp.bfloat16)
     joined_in[me] = joined_out[me]
 
     def j_copy(k):
@@ -228,29 +262,28 @@
 
     lax.fori_loop(1, n, start_joined, 0)
     lax.fori_loop(1, n, wait_joined, 0)
-    for j in range(n):
-        joined_2d[j * local : (j + 1) * local, :] = joined_in[j].astype(jnp.float32)
-
-    pieces = columns // HALF
-    shape = (local * SLOTS, n * local)
+    width = pieces * local
+    if width % 16 == 0:
+        moved = joined_in[...].reshape(n * width, HALF)
+    else:
+        for j in range(n):
+            joined_2d[j * width : (j + 1) * width, :] = joined_in[j].astype(jnp.float32)
+        moved = joined_2d[...].astype(jnp.bfloat16)
+
+    shape = (local * SLOTS, n * width)
     to_row = lax.broadcasted_iota(jnp.int32, shape, 0)
-    from_row = lax.broadcasted_iota(jnp.int32, shape, 1)
-    same_row = to_row // SLOTS == from_row % local
-    to_piece = 2 * (to_row % SLOTS)
-    from_piece = pieces * (from_row // local)
+    source = lax.broadcasted_iota(jnp.int32, shape, 1)
+    same_row = to_row // SLOTS == source % local
     halves = []
     for part in range(2):
-        half = jnp.zeros((local * SLOTS, HALF), jnp.float32)
-        for piece in range(pieces):
-            if pieces % 2 == 0 and piece % 2 != part:
-                continue
-            chosen = same_row & (from_piece + piece == to_piece + part)
-            half += jnp.dot(
+        chosen = same_row & (source // local == 2 * (to_row % SLOTS) + part)
+        halves.append(
+            jnp.dot(
                 jnp.where(chosen, 1.0, 0.0).astype(jnp.bfloat16),
-                joined_2d[:, piece * HALF : (piece + 1) * HALF].astype(jnp.bfloat16),
+                moved,
                 preferred_element_type=jnp.float32,
             )
-        halves.append(half)
+        )
 
     k_copy.wait()
     v_copy.wait()
@@ -297,23 +330,34 @@
         stacked,
         preferred_element_type=jnp.float32,
     )
+    quarter = att.shape[2]
+    per_quarter = quarter // HALF
     for h in range(HQ):
-        att[me, :, h * DH : (h + 1) * DH] = heads_first[
-            h * local : (h + 1) * local, :
-        ].astype(jnp.bfloat16)
-
-    spread = Gather(n, me, att, a_send, a_recv)
+        for part in range(2):
+            at, place = (2 * h + part) // per_quarter, (2 * h + part) % per_quarter
+            att_f32[at * local : (at + 1) * local, place * HALF : (place + 1) * HALF] = heads_first[
+                h * local : (h + 1) * local, part * HALF : (part + 1) * HALF
+            ]
+    att[me] = att_f32[...].astype(jnp.bfloat16)
+
+    spread = Gather(n, me, att, 1, a_send, a_recv)
     spread.run(lambda slab: None)
 
-    for j in range(n):
-        att_2d[j * local : (j + 1) * local, :] = att[j].astype(jnp.float32)
+    height = att.shape[1]
+    gathered = att[...].reshape(n * height, quarter)
+    shape = (rows, n * height)
+    to_row = lax.broadcasted_iota(jnp.int32, shape, 0)
+    source = lax.broadcasted_iota(jnp.int32, shape, 1)
+    same_row = (to_row // local == source // height) & (to_row % local == source % local)
     for i, copy in enumerate(wo_copies):
+        chosen = same_row & (source % height // local == i)
+        part = jnp.dot(
+            jnp.where(chosen, 1.0, 0.0).astype(jnp.bfloat16),
+            gathered,
+            preferred_element_type=jnp.float32,
+        ).astype(jnp.bfloat16)
         copy.wait()
-        product = jnp.dot(
-            att_2d[:, i * depth : (i + 1) * depth].astype(jnp.bfloat16),
-            wo_v[i],
-            preferred_element_type=jnp.float32,
-        )
+        product = jnp.dot(part, wo_v[i], preferred_element_type=jnp.float32)
         if i == 0:
             total[...] = product
         elif i < OUT_CHUNKS - 1:
@@ -344,7 +388,7 @@
     smem = pl.BlockSpec(memory_space=pltpu.SMEM)
     hbm = pl.BlockSpec(memory_space=pl.ANY)
     dma = pltpu.SemaphoreType.DMA
-    sends = n_gather_sends(n)
+    pieces = columns // HALF
     return pl.pallas_call(
         functools.partial(kernel, n),
         out_shape=jax.ShapeDtypeStruct((rows, width), bf16),
@@ -355,14 +399,15 @@
             pltpu.VMEM((n, rows, features), bf16),
             pltpu.VMEM((n, features, columns), bf16),
             pltpu.VMEM((rows, columns), f32),
-            pltpu.VMEM((n, local, columns), bf16),
-            pltpu.VMEM((n, local, columns), bf16),
-            pltpu.VMEM((rows, columns), f32),
+            pltpu.VMEM((n, pieces * local, HALF), f32),
+            pltpu.VMEM((n, pieces * local, HALF), bf16),
+            pltpu.VMEM((n, pieces * local, HALF), bf16),
+            pltpu.VMEM((n * pieces * local, HALF), f32),
             pltpu.VMEM((local, context, DH), bf16),
             pltpu.VMEM((local, context, DH), bf16),
             pltpu.VMEM((local * SLOTS, DH), f32),
-            pltpu.VMEM((n, local, inner), bf16),
-            pltpu.VMEM((rows, inner), f32),
+            pltpu.VMEM((OUT_CHUNKS * local, inner // OUT_CHUNKS), f32),
+            pltpu.VMEM((n, OUT_CHUNKS * local, inner // OUT_CHUNKS), bf16),
             pltpu.VMEM((OUT_CHUNKS, inner // OUT_CHUNKS, width), bf16),
             pltpu.VMEM((rows, width), f32),
             dma((n,)),
@@ -370,12 +415,12 @@
             dma((OUT_CHUNKS,)),
             dma((n,)),
             dma((n,)),
-            dma((sends,)),
+            dma((4, n, X_CHUNKS)),
+            dma((n, X_CHUNKS)),
             dma((n,)),
             dma((n,)),
-            dma((n,)),
-            dma((sends,)),
-            dma((n,)),
+            dma((4, n, 1)),
+            dma((n, 1)),
         ],
         compiler_params=pltpu.CompilerParams(
             collective_id=0, has_side_effects=True, vmem_limit_bytes=60 * 1024 * 1024

time: 73.1 us -> 61.7 us (0.84)
  Pallas kernels: 68.7 us -> 57.2 us
    pallas_call x1, Pallas kernels: 68.7 us -> 57.2 us  [shards(): pl.pallas_call(functools.partial(kernel, n), out_shape=jax.ShapeDtypeStru...]
where the time goes in v2:
time: 61.7 us; the launch traced here: 61.5 us
  Pallas kernels  57.2 us (93%)
  local copies, waits for them, and re-layouts  2.87 us (5%)
  other arithmetic  1.36 us (2%)
    pallas_call x1, Pallas kernels, shards(): pl.pallas_call(functools.partial(kernel, n), out_shape=jax.ShapeDtypeStru...  57.2 us
    unnamed x1, local copies, waits for them, and re-layouts  1.58 us
    reshape x1, local copies, waits for them, and re-layouts, shards(): norm_gain.reshape(1, features)  1.28 us

profile of v2, /device:TPU:1, one launch (start us, length us, event | category | flops | bytes accessed | tf_op | source)
XLA Modules:
  0.0 61.5 jit_solution(5265982900501502181)
XLA Ops:
  0.0 0.7 %convert_element_type.3 = f32[4]{0:T(128)S(1)} convert(s32[4]{0:T(128)} %param.14) | non-fusion elementwise | flops 4 | bytes 32 | tf_op jit(solution)/shard_map/convert_element_type | solution.py:385
  0.7 0.7 %multiply_sine_fusion = (f32[4,128]{1,0:T(4,128)}, f32[4,128]{1,0:T(4,128)}) fusion(f32[128]{0:T(128)S(1)} %multiply_power_fusion, f32[4]{0:T(128)S(1)} %convert_element_type.3), kind=kLoop, calls=%fused_computation | loop fusion | flops 512 | bytes 4624 | tf_op jit(solution)/shard_map/sin | solution.py:430
  1.4 1.3 %reshape.9.gain_ref = bf16[1,1152]{1,0:T(2,128)(2,1)} reshape(bf16[1152]{0:T(1024)(128)(2,1)} %param.9) | data formatting | bytes 4608 | tf_op jit(solution)/shard_map/reshape | solution.py:429
  2.6 57.2 %shard_map.82 = bf16[64,1152]{1,0:T(8,128)(2,1)} custom-call(bf16[64,1152]{1,0:T(8,128)(2,1)} %x_ref.1, bf16[1,1152]{1,0:T(2,128)(2,1)} %reshape.9.gain_ref, bf16[18432,512]{1,0:T(8,128)(2,1)} %w_hbm.1, bf16[4,1024,256]{2,1,0:T(8,128)(2,1)} %k_hbm.1, bf16[4,1024,256]{2,1,0:T(8,128)(2,1)} %v_hbm.1, s32[4]{0:T(128)} %len_ref.1, ...), custom_call_target="tpu_custom_call" | custom-call | tf_op jit(solution)/shard_map/pallas_call | solution.py:392
  59.9 1.6 %copy.10 = bf16[64,1152]{1,0:T(8,128)(2,1)} copy(bf16[64,1152]{1,0:T(8,128)(2,1)} %shard_map.82) | data formatting | bytes 294912
  (1 shorter events, 0.0 us)
